TPU v7x, 256 devices: a whole 4x4x8 slice. The times are simulated.
256 devices in a mesh: cube: 8 (over z), front: 32 (over x, y, core).
Axes of the slice: x: 4, y: 4, z: 8, core: 2. Of those that a mesh axis runs over, the one named last changes fastest.
Arguments:
- right_sides: float32 [3, 8, 2048, 128], P(None, 'cube', 'front'), may hold values from -6 to 6
- inverse_leaf: float32 [8, 2048, 2048], P('cube', 'front'), may hold values from -2 to 2, as said below
- inverse_mid: float32 [8, 2048, 4096], P('cube', 'front'), may hold values from -2 to 2, as said below
- inverse_top: float32 [8, 2048, 8192], P('cube', 'front'), may hold values from -2 to 2, as said below
- coupling_mid: float32 [8, 2048, 4096], P('cube', 'front'), may hold values from -0.1875 to 0.1875
- coupling_top: float32 [8, 2048, 8192], P('cube', 'front'), may hold values from -0.125 to 0.125
- pattern_mid: int32 [8, 32, 64], P('cube', 'front'), may hold values 0 or 1
- pattern_top: int32 [8, 32, 128], P('cube', 'front'), may hold values 0 or 1
Outputs:
- solution: float32 [3, 8, 2048, 128], P(None, 'cube', 'front')
Inputs may be any that keep to these rules, and one draw needn't show every extreme that they name: `inverse_leaf`: each block is the inverse of a lower triangular diagonal block: zero above the diagonal of the separator's row order, diagonal 1 to 2. `inverse_mid`: as inverse_leaf. `inverse_top`: as inverse_leaf.
All inputs are finite; a program needn't handle non-finite values. No bound on the sum of `pattern_mid` or of `pattern_top` on one device may be relied on, other than what follows from the above.
Results may differ from a plain program's by a relative error of at most 0.00013.
Values sent between devices are 32-bit elements; how exact they have to be, the bound alone decides.
A program may use at most 64 MiB of HBM per device.

v0:
```python
import jax
import jax.numpy as jnp
from jax import lax
from jax.sharding import PartitionSpec as P

TILE = 64


def from_behind(array, axis, by):
    devices = lax.axis_size(axis)
    pairs = [(i, i + by) for i in range(devices) if 0 <= i + by < devices]
    return lax.ppermute(array, axis, pairs)


def masked(coupling, pattern):
    keep_rows = jnp.repeat(pattern[0], TILE, axis=0)
    keep_all = jnp.repeat(keep_rows, TILE, axis=1)
    return coupling[0] * keep_all.astype(jnp.float32)


def members_of(local_rows, count, cube_pos):
    if count == 1:
        return local_rows[None]
    copies = []
    for distance in range(-(count - 1), count):
        if distance == 0:
            copies.append(local_rows)
        else:
            copies.append(from_behind(local_rows, "cube", distance))
    every_copy = jnp.stack(copies, 0)
    member_pos = cube_pos % count
    wanted = member_pos - jnp.arange(count, dtype=jnp.int32) + (count - 1)
    return jnp.take(every_copy, wanted, axis=0)


def gathered_product(matrix, stacked):
    count = stacked.shape[0]
    height = matrix.shape[0]
    member_width = matrix.shape[1] // count
    shaped = matrix.reshape(height, count, member_width)
    return jnp.einsum(
        "rms,msn->rn",
        shaped,
        lax.all_gather(stacked, "front", axis=1, tiled=True),
        precision=lax.Precision.HIGHEST,
        preferred_element_type=jnp.float32,
    )


def spread_back(matrix, local_rows, count, cube_pos):
    height = matrix.shape[0]
    member_width = matrix.shape[1] // count
    shaped = matrix.reshape(height, count, member_width)
    summed = lax.psum_scatter(
        jnp.einsum(
            "rms,rn->smn",
            shaped,
            local_rows,
            precision=lax.Precision.HIGHEST,
            preferred_element_type=jnp.float32,
        ),
        "front",
        scatter_dimension=0,
        tiled=True,
    )
    if count == 1:
        return summed[:, 0]
    start_pos = cube_pos // count * count
    zeros_all = jnp.zeros((height, lax.axis_size("cube"), summed.shape[2]), jnp.float32)
    placed = lax.dynamic_update_slice_in_dim(zeros_all, summed, start_pos, 1)
    return lax.psum_scatter(placed, "cube", scatter_dimension=1, tiled=True)[:, 0]


def local(
    right_sides,
    inverse_leaf,
    inverse_mid,
    inverse_top,
    coupling_mid,
    coupling_top,
    pattern_mid,
    pattern_top,
):
    cube_pos = lax.axis_index("cube")
    block_mid = masked(coupling_mid, pattern_mid)
    block_top = masked(coupling_top, pattern_top)
    inv_leaf = inverse_leaf[0]
    inv_mid = inverse_mid[0]
    inv_top = inverse_top[0]
    sides = right_sides[:, 0]
    solved_leaf = gathered_product(inv_leaf, members_of(sides[0], 1, cube_pos))
    update_mid = gathered_product(block_mid, members_of(solved_leaf, 2, cube_pos))
    solved_mid = gathered_product(inv_mid, members_of(sides[1] - update_mid, 2, cube_pos))
    update_top = gathered_product(block_top, members_of(solved_mid, 4, cube_pos))
    solved_top = gathered_product(inv_top, members_of(sides[2] - update_top, 4, cube_pos))
    back_top = spread_back(inv_top, solved_top, 4, cube_pos)
    carry_mid = spread_back(block_top, back_top, 4, cube_pos)
    back_mid = spread_back(inv_mid, solved_mid - carry_mid, 2, cube_pos)
    carry_leaf = spread_back(block_mid, back_mid, 2, cube_pos)
    back_leaf = spread_back(inv_leaf, solved_leaf - carry_leaf, 1, cube_pos)
    result = jnp.stack([back_leaf, back_mid, back_top])
    return result[:, None]


def solution(mesh):
    return jax.shard_map(
        local,
        mesh=mesh,
        in_specs=(
            P(None, "cube", "front", None),
            P("cube", "front", None),
            P("cube", "front", None),
            P("cube", "front", None),
            P("cube", "front", None),
            P("cube", "front", None),
            P("cube", "front", None),
            P("cube", "front", None),
        ),
        out_specs=P(None, "cube", "front", None),
        check_vma=False,
    )
```

profile of v0, /device:TPU:1, one launch (start us, length us, event | category | flops | bytes accessed | tf_op | source)
XLA Modules:
  0.0 978.5 jit_solution(17281980897856328411)
XLA Ops:
  8.2 53.8 %all-gather.15.cloned.1.call-done = f32[1,1,2048,128]{3,2,1,0:T(8,128)} async-done(((f32[1,1,64,128]{3,2,1,0:T(8,128)}), f32[1,1,2048,128]{3,2,1,0:T(8,128)}) %all-gather.15.cloned.1.call-update) | async-done | bytes 1048592 | tf_op jit(solution)/shard_map/all_gather | solution.py:44
  72.8 50.3 %all-gather.7.cloned.1.call-done = f32[2,2048,128]{2,1,0:T(8,128)} async-done(((f32[2,64,128]{2,1,0:T(8,128)}), f32[2,2048,128]{2,1,0:T(8,128)}) %all-gather.7.cloned.1.call-update) | async-done | bytes 2097168 | tf_op jit(solution)/shard_map/all_gather | solution.py:44
  135.2 50.4 %all-gather.9.cloned.1.call-done = f32[2,2048,128]{2,1,0:T(8,128)} async-done(((f32[2,64,128]{2,1,0:T(8,128)}), f32[2,2048,128]{2,1,0:T(8,128)}) %all-gather.9.cloned.1.call-update) | async-done | bytes 2097168 | tf_op jit(solution)/shard_map/all_gather | solution.py:44
  197.0 5.2 collective-permute-start.8
  202.3 6.6 collective-permute-start.9
  214.6 50.3 %all-gather.11.cloned.1.call-done = f32[4,2048,128]{2,1,0:T(8,128)} async-done(((f32[4,64,128]{2,1,0:T(8,128)}), f32[4,2048,128]{2,1,0:T(8,128)}) %all-gather.11.cloned.1.call-update) | async-done | bytes 4194320 | tf_op jit(solution)/shard_map/all_gather | solution.py:44
  264.9 5.9 fusion.7
  278.7 5.3 collective-permute-start.14
  284.0 6.6 collective-permute-start.15
  296.2 50.5 %all-gather.13.cloned.1.call-done = f32[4,2048,128]{2,1,0:T(8,128)} async-done(((f32[4,64,128]{2,1,0:T(8,128)}), f32[4,2048,128]{2,1,0:T(8,128)}) %all-gather.13.cloned.1.call-update) | async-done | bytes 4194320 | tf_op jit(solution)/shard_map/all_gather | solution.py:44
  346.7 5.9 fusion.2
  352.7 8.4 convolution_bitcast_fusion.1
  361.4 86.9 %reduce-scatter.10.cloned.1.call-done = f32[64,4,128]{2,0,1:T(8,128)} async-done(((f32[2048,4,128]{2,0,1:T(8,128)}), f32[64,4,128]{2,0,1:T(8,128)}) %reduce-scatter.10.cloned.1.call-update) | async-done | bytes 131088 | tf_op jit(solution)/shard_map/reduce_scatter | solution.py:54
  454.3 28.8 %reduce-scatter.12.cloned.1.call-done = f32[64,1,128]{2,0,1:T(8,128)} async-done(((f32[64,8,128]{2,0,1:T(8,128)}), f32[64,1,128]{2,0,1:T(8,128)}) %reduce-scatter.12.cloned.1.call-update) | async-done | bytes 32784 | tf_op jit(solution)/shard_map/reduce_scatter | solution.py:71
  483.1 9.2 convolution_bitcast_fusion
  492.4 92.1 %reduce-scatter.14.cloned.1.call-done = f32[64,4,128]{2,0,1:T(8,128)} async-done(((f32[2048,4,128]{2,0,1:T(8,128)}), f32[64,4,128]{2,0,1:T(8,128)}) %reduce-scatter.14.cloned.1.call-update) | async-done | bytes 131088 | tf_op jit(solution)/shard_map/reduce_scatter | solution.py:54
  586.2 33.2 %reduce-scatter.16.cloned.1.call-done = f32[64,1,128]{2,0,1:T(8,128)} async-done(((f32[64,8,128]{2,0,1:T(8,128)}), f32[64,1,128]{2,0,1:T(8,128)}) %reduce-scatter.16.cloned.1.call-update) | async-done | bytes 32784 | tf_op jit(solution)/shard_map/reduce_scatter | solution.py:71
  619.4 5.7 convolution_bitcast_fusion.3
  625.4 88.9 %reduce-scatter.18.cloned.1.call-done = f32[64,2,128]{2,0,1:T(8,128)} async-done(((f32[2048,2,128]{2,0,1:T(8,128)}), f32[64,2,128]{2,0,1:T(8,128)}) %reduce-scatter.18.cloned.1.call-update) | async-done | bytes 65552 | tf_op jit(solution)/shard_map/reduce_scatter | solution.py:54
  717.1 32.6 %reduce-scatter.20.cloned.1.call-done = f32[64,1,128]{2,0,1:T(8,128)} async-done(((f32[64,8,128]{2,0,1:T(8,128)}), f32[64,1,128]{2,0,1:T(8,128)}) %reduce-scatter.20.cloned.1.call-update) | async-done | bytes 32784 | tf_op jit(solution)/shard_map/reduce_scatter | solution.py:71
  749.6 5.7 convolution_bitcast_fusion.2
  755.5 88.5 %reduce-scatter.22.cloned.1.call-done = f32[64,2,128]{2,0,1:T(8,128)} async-done(((f32[2048,2,128]{2,0,1:T(8,128)}), f32[64,2,128]{2,0,1:T(8,128)}) %reduce-scatter.22.cloned.1.call-update) | async-done | bytes 65552 | tf_op jit(solution)/shard_map/reduce_scatter | solution.py:54
  845.6 33.3 %reduce-scatter.24.cloned.1.call-done = f32[64,1,128]{2,0,1:T(8,128)} async-done(((f32[64,8,128]{2,0,1:T(8,128)}), f32[64,1,128]{2,0,1:T(8,128)}) %reduce-scatter.24.cloned.1.call-update) | async-done | bytes 32784 | tf_op jit(solution)/shard_map/reduce_scatter | solution.py:71
  882.5 87.8 %reduce-scatter.26.cloned.1.call-done = f32[64,1,128]{2,0,1:T(8,128)} async-done(((f32[2048,1,128]{2,0,1:T(8,128)}), f32[64,1,128]{2,0,1:T(8,128)}) %reduce-scatter.26.cloned.1.call-update) | async-done | bytes 32784 | tf_op jit(solution)/shard_map/reduce_scatter | solution.py:54
  (154 shorter events, 72.3 us)
Async XLA Ops:
  6.5 55.4 %all-gather.15.cloned.1.call-start = ((), (), s32[]{:S(2)}) async-start(), calls=%async_computation.22 | async-start | bytes 1081344 | tf_op jit(solution)/shard_map/all_gather | solution.py:44
  8.1 115.0 %all-gather.7.cloned.1.call-start = ((), (), s32[]{:S(2)}) async-start(), calls=%async_computation.9 | async-start | bytes 2162688 | tf_op jit(solution)/shard_map/all_gather | solution.py:44
  71.5 114.1 %all-gather.9.cloned.1.call-start = ((), (), s32[]{:S(2)}) async-start(), calls=%async_computation.10 | async-start | bytes 2162688 | tf_op jit(solution)/shard_map/all_gather | solution.py:44
  134.2 130.7 %all-gather.11.cloned.1.call-start = ((), (), s32[]{:S(2)}) async-start(), calls=%async_computation.11 | async-start | bytes 4325376 | tf_op jit(solution)/shard_map/all_gather | solution.py:44
  189.1 13.2 %collective-permute-start.4 = (f32[64,128]{1,0:T(8,128)S(1)}, f32[64,128]{1,0:T(8,128)S(1)}, u32[]{:S(2)}, u32[]{:S(2)}) collective-permute-start(f32[64,128]{1,0:T(8,128)S(1)} %bitcast.110), channel_id=1, source_target_pairs={{96,0},{128,32},{160,64},{192,96},{224,128},{97,1},{129,33},{161,6... | collective-permute-start | bytes 98312 | tf_op jit(solution)/shard_map/ppermute | solution.py:12
  190.4 18.5 %collective-permute-start.5 = (f32[64,128]{1,0:T(8,128)S(1)}, f32[64,128]{1,0:T(8,128)S(1)}, u32[]{:S(2)}, u32[]{:S(2)}) collective-permute-start(f32[64,128]{1,0:T(8,128)S(1)} %bitcast.111), channel_id=1, source_target_pairs={{64,0},{96,32},{128,64},{160,96},{192,128},{224,160},{65,1},{97,33... | collective-permute-start | bytes 98312 | tf_op jit(solution)/shard_map/ppermute | solution.py:12
  191.7 17.3 %collective-permute-start.6 = (f32[64,128]{1,0:T(8,128)S(1)}, f32[64,128]{1,0:T(8,128)S(1)}, u32[]{:S(2)}, u32[]{:S(2)}) collective-permute-start(f32[64,128]{1,0:T(8,128)S(1)} %bitcast.112), channel_id=1, source_target_pairs={{32,0},{64,32},{96,64},{128,96},{160,128},{192,160},{224,192},{33,... | collective-permute-start | bytes 98312 | tf_op jit(solution)/shard_map/ppermute | solution.py:12
  193.0 16.0 %collective-permute-start.7 = (f32[64,128]{1,0:T(8,128)S(1)}, f32[64,128]{1,0:T(8,128)S(1)}, u32[]{:S(2)}, u32[]{:S(2)}) collective-permute-start(f32[64,128]{1,0:T(8,128)S(1)} %bitcast.113), channel_id=1, source_target_pairs={{0,32},{32,64},{64,96},{96,128},{128,160},{160,192},{192,224},{1,3... | collective-permute-start | bytes 98312 | tf_op jit(solution)/shard_map/ppermute | solution.py:12
  197.0 12.0 %collective-permute-start.8 = (f32[64,128]{1,0:T(8,128)S(1)}, f32[64,128]{1,0:T(8,128)S(1)}, u32[]{:S(2)}, u32[]{:S(2)}) collective-permute-start(f32[64,128]{1,0:T(8,128)S(1)} %bitcast.114), channel_id=1, source_target_pairs={{0,64},{32,96},{64,128},{96,160},{128,192},{160,224},{1,65},{33,97... | collective-permute-start | bytes 98312 | tf_op jit(solution)/shard_map/ppermute | solution.py:12
  211.3 135.4 %all-gather.13.cloned.1.call-start = ((), (), s32[]{:S(2)}) async-start(), calls=%async_computation.12 | async-start | bytes 4325376 | tf_op jit(solution)/shard_map/all_gather | solution.py:44
  270.8 13.2 %collective-permute-start.10 = (f32[64,128]{1,0:T(8,128)S(1)}, f32[64,128]{1,0:T(8,128)S(1)}, u32[]{:S(2)}, u32[]{:S(2)}) collective-permute-start(f32[64,128]{1,0:T(8,128)S(1)} %fusion.7), channel_id=1, source_target_pairs={{96,0},{128,32},{160,64},{192,96},{224,128},{97,1},{129,33},{161,6... | collective-permute-start | bytes 98312 | tf_op jit(solution)/shard_map/ppermute | solution.py:12
  272.1 18.5 %collective-permute-start.11 = (f32[64,128]{1,0:T(8,128)S(1)}, f32[64,128]{1,0:T(8,128)S(1)}, u32[]{:S(2)}, u32[]{:S(2)}) collective-permute-start(f32[64,128]{1,0:T(8,128)S(1)} %fusion.7), channel_id=1, source_target_pairs={{64,0},{96,32},{128,64},{160,96},{192,128},{224,160},{65,1},{97,33... | collective-permute-start | bytes 98312 | tf_op jit(solution)/shard_map/ppermute | solution.py:12
  273.4 17.3 %collective-permute-start.12 = (f32[64,128]{1,0:T(8,128)S(1)}, f32[64,128]{1,0:T(8,128)S(1)}, u32[]{:S(2)}, u32[]{:S(2)}) collective-permute-start(f32[64,128]{1,0:T(8,128)S(1)} %fusion.7), channel_id=1, source_target_pairs={{32,0},{64,32},{96,64},{128,96},{160,128},{192,160},{224,192},{33,... | collective-permute-start | bytes 98312 | tf_op jit(solution)/shard_map/ppermute | solution.py:12
  274.7 16.0 %collective-permute-start.13 = (f32[64,128]{1,0:T(8,128)S(1)}, f32[64,128]{1,0:T(8,128)S(1)}, u32[]{:S(2)}, u32[]{:S(2)}) collective-permute-start(f32[64,128]{1,0:T(8,128)S(1)} %fusion.7), channel_id=1, source_target_pairs={{0,32},{32,64},{64,96},{96,128},{128,160},{160,192},{192,224},{1,3... | collective-permute-start | bytes 98312 | tf_op jit(solution)/shard_map/ppermute | solution.py:12
  278.7 12.0 %collective-permute-start.14 = (f32[64,128]{1,0:T(8,128)S(1)}, f32[64,128]{1,0:T(8,128)S(1)}, u32[]{:S(2)}, u32[]{:S(2)}) collective-permute-start(f32[64,128]{1,0:T(8,128)S(1)} %fusion.7), channel_id=1, source_target_pairs={{0,64},{32,96},{64,128},{96,160},{128,192},{160,224},{1,65},{33,97... | collective-permute-start | bytes 98312 | tf_op jit(solution)/shard_map/ppermute | solution.py:12
  293.0 155.2 %reduce-scatter.10.cloned.1.call-start = ((), (), s32[]{:S(2)}) async-start(), calls=%async_computation.13 | async-start | bytes 4325376 | tf_op jit(solution)/shard_map/reduce_scatter | solution.py:54
  361.1 122.0 %reduce-scatter.12.cloned.1.call-start = ((), (), s32[]{:S(2)}) async-start(), calls=%async_computation.14 | async-start | bytes 294912 | tf_op jit(solution)/shard_map/reduce_scatter | solution.py:71
  449.9 134.6 %reduce-scatter.14.cloned.1.call-start = ((), (), s32[]{:S(2)}) async-start(), calls=%async_computation.15 | async-start | bytes 4325376 | tf_op jit(solution)/shard_map/reduce_scatter | solution.py:54
  492.3 127.1 %reduce-scatter.16.cloned.1.call-start = ((), (), s32[]{:S(2)}) async-start(), calls=%async_computation.16 | async-start | bytes 294912 | tf_op jit(solution)/shard_map/reduce_scatter | solution.py:71
  586.2 128.0 %reduce-scatter.18.cloned.1.call-start = ((), (), s32[]{:S(2)}) async-start(), calls=%async_computation.17 | async-start | bytes 2162688 | tf_op jit(solution)/shard_map/reduce_scatter | solution.py:54
  625.2 124.5 %reduce-scatter.20.cloned.1.call-start = ((), (), s32[]{:S(2)}) async-start(), calls=%async_computation.18 | async-start | bytes 294912 | tf_op jit(solution)/shard_map/reduce_scatter | solution.py:71
  715.8 128.2 %reduce-scatter.22.cloned.1.call-start = ((), (), s32[]{:S(2)}) async-start(), calls=%async_computation.19 | async-start | bytes 2162688 | tf_op jit(solution)/shard_map/reduce_scatter | solution.py:54
  755.4 123.5 %reduce-scatter.24.cloned.1.call-start = ((), (), s32[]{:S(2)}) async-start(), calls=%async_computation.20 | async-start | bytes 294912 | tf_op jit(solution)/shard_map/reduce_scatter | solution.py:71
  845.6 124.7 %reduce-scatter.26.cloned.1.call-start = ((), (), s32[]{:S(2)}) async-start(), calls=%async_computation.21 | async-start | bytes 1081344 | tf_op jit(solution)/shard_map/reduce_scatter | solution.py:54
  (22 other events, 1216.3 us)
Sparse Core Ops, SparseCore 0:
  9.9 52.0 all-gather.14
  71.7 51.3 all-gather.6
  134.3 51.2 all-gather.8
  211.4 53.4 all-gather.10
  293.1 53.6 all-gather.12
  361.2 86.9 reduce-scatter.9
  450.9 32.1 reduce-scatter.11
  492.5 92.0 reduce-scatter.13
  587.2 32.1 reduce-scatter.15
  625.3 88.9 reduce-scatter.17
  716.7 32.8 reduce-scatter.19
  755.5 88.4 reduce-scatter.21
  846.6 32.2 reduce-scatter.23
  882.6 87.6 reduce-scatter.25
where the time goes:
time: 986 us; the launch traced here: 978 us
  waiting for transfers between devices  831 us (84%)
  matrix products  53.5 us (5%)
  starting transfers between devices  51.8 us (5%)
  local copies, waits for them, and re-layouts  21.7 us (2%)
  between operations  14.2 us (1%)
    reduce_scatter x5, waiting for transfers between devices, spread_back(): lax.psum_scatter(jnp.einsum('rms,rn->smn', shaped, local_rows, precision=...  444 us
    all_gather x5, waiting for transfers between devices, gathered_product(): lax.all_gather(stacked, 'front', axis=1, tiled=True)  255 us
    reduce_scatter x4, waiting for transfers between devices, spread_back(): lax.psum_scatter(placed, 'cube', scatter_dimension=1, tiled=True)[:, 0]  128 us
    ppermute x16, starting transfers between devices, from_behind(): return lax.ppermute(array, axis, pairs)  50.1 us
    dot_general x5, matrix products, spread_back(): jnp.einsum('rms,rn->smn', shaped, local_rows, precision=lax.Precision.HIG...  32.6 us
    dot_general x5, matrix products, gathered_product(): jnp.einsum('rms,msn->rn', shaped, lax.all_gather(stacked, 'front', axis=1...  20.8 us
  transfers between devices with their start and end apart: 30, of which 18 were waited for; matrix products, arithmetic and copies ran while one was open for 1% of the time, Pallas kernels for 0%

commit v1 on v0

v1 whole, which is shorter than its diff:
```python
import functools

import jax
import jax.numpy as jnp
from jax import lax
from jax.experimental import pallas as pl
from jax.experimental.pallas import tpu as pltpu
from jax.sharding import PartitionSpec as P

MESH = pl.DeviceIdType.MESH
SIDE = 4
ROWS = 64
COLS = 128
HALF = ROWS // 2
BLOCK = SIDE * SIDE * ROWS
FIRST = (0, 1, 3, 5, 9)
COUNT = (1, 2, 2, 4, 4)
BLOCKS = 13
F32, BF16 = jnp.float32, jnp.bfloat16


def split(values):
    high = values.astype(BF16)
    low = (values - high.astype(F32)).astype(BF16)
    return high, low


class Copies:
    def __init__(self, send, recv):
        self.send, self.recv, self.used, self.sent = send, recv, 0, []

    def slot(self):
        self.used += 1
        return self.used - 1

    def start(self, slot, src, dst, device):
        copy = pltpu.make_async_remote_copy(
            src_ref=src, dst_ref=dst, send_sem=self.send.at[slot], recv_sem=self.recv.at[slot],
            device_id=device, device_id_type=MESH,
        )
        copy.start()
        self.sent.append(copy)

    def arrived(self, slot, dst, device):
        pltpu.make_async_remote_copy(
            src_ref=dst, dst_ref=dst, send_sem=self.send.at[slot], recv_sem=self.recv.at[slot],
            device_id=device, device_id_type=MESH,
        ).wait_recv()

    def finish(self):
        for copy in self.sent:
            copy.wait_send()


def kernel(
    sides, leaf, mid, top, cmid, ctop, pmid, ptop, out,
    raw_leaf, raw_cmid, raw_mid, raw_ctop, raw_top, halves, sibling_half, rows_cat, cols_cat,
    gathered, partial, recv_first, recv_second, reduced, recv_cube, mine, cross, local_sem, send, recv,
):
    cube = lax.axis_index("cube")
    front = lax.axis_index("front")
    core = lax.rem(front, 2)
    ypos = lax.rem(front // 2, SIDE)
    xpos = front // (2 * SIDE)

    def at(x, y, z, c):
        return (z, (x * SIDE + y) * 2 + c)

    def along_x(by):
        return at(lax.rem(xpos + by, SIDE), ypos, cube, core)

    def along_y(by):
        return at(xpos, lax.rem(ypos + by, SIDE), cube, core)

    def along_z(by, members):
        member = lax.rem(cube, members)
        return at(xpos, ypos, cube - member + lax.rem(member + by, members), core)

    sibling = at(xpos, ypos, cube, 1 - core)
    copies = Copies(send, recv)

    raws = (raw_leaf, raw_cmid, raw_mid, raw_ctop, raw_top)
    loads = []
    for k, (src, dst) in enumerate(zip((leaf, cmid, mid, ctop, top), raws)):
        load = pltpu.make_async_copy(src.at[0], dst, local_sem.at[k])
        load.start()
        loads.append(load)

    barrier = pltpu.get_barrier_semaphore()
    peers = [sibling]
    for by in range(1, SIDE):
        peers += [along_x(by), along_y(by), along_z(by, 4)]
    for peer in peers:
        pl.semaphore_signal(barrier, inc=1, device_id=peer, device_id_type=MESH)
    pl.semaphore_wait(barrier, len(peers))

    lane = lax.broadcasted_iota(jnp.int32, (ROWS, 128), 1)
    first_half = lane < ROWS

    half_slots = {}

    def halve(k, pattern):
        loads[k].wait()

        def one(m, carry):
            for i in range(BLOCK // 128):
                at_column = pl.multiple_of(m * (2 * BLOCK) + i * 256, 256)
                left = raws[k][:, pl.ds(at_column, 128)]
                right = raws[k][:, pl.ds(at_column + 128, 128)]
                low = jnp.where(first_half, left, pltpu.roll(right, ROWS, 1))
                high = jnp.where(first_half, pltpu.roll(left, ROWS, 1), right)
                if pattern is not None:
                    tile = m * (2 * BLOCK // ROWS) + 4 * i
                    keep = [pattern[0, 0, tile + j].astype(F32) for j in range(4)]
                    low = low * jnp.where(first_half, keep[0], keep[2])
                    high = high * jnp.where(first_half, keep[1], keep[3])
                halves[0, FIRST[k] + m, :, i * 128 : (i + 1) * 128] = low
                halves[1, FIRST[k] + m, :, i * 128 : (i + 1) * 128] = high
            return carry

        lax.fori_loop(0, COUNT[k], one, 0)
        where = pl.ds(FIRST[k], COUNT[k])
        half_slots[k] = copies.slot()
        copies.start(half_slots[k], halves.at[1 - core, where], sibling_half.at[where], sibling)

    def fill_rows(k):
        where = pl.ds(FIRST[k], COUNT[k])
        copies.arrived(half_slots[k], sibling_half.at[where], sibling)

        def one(m, carry):
            blk = FIRST[k] + m
            for first, source in ((0, halves[core, blk]), (ROWS, sibling_half[blk])):
                high, low = split(source)
                rows_cat[blk, first : first + ROWS] = high
                rows_cat[blk, 2 * ROWS + first : 3 * ROWS + first] = low
            return carry

        lax.fori_loop(0, COUNT[k], one, 0)

    def fill_cols(k):
        def one(m, carry):
            blk = FIRST[k] + m
            for i in range(BLOCK // 128):
                part = slice(i * 128, (i + 1) * 128)
                both = jnp.concatenate([halves[core, blk, :, part], sibling_half[blk, :, part]], 0)
                high, low = split(both.T)
                cols_cat[blk, part, :128] = high
                cols_cat[blk, part, 128:] = low
            return carry

        lax.fori_loop(0, COUNT[k], one, 0)

    def gather_product(k, shard, early, late):
        first, members = FIRST[k], COUNT[k]
        member = lax.rem(cube, members)
        gathered[first, xpos, ypos] = shard
        groups = [(first, 1)] + ([(first + 1, members - 1)] if members > 1 else [])
        z_slots = [copies.slot() for _ in range(1, members)]
        for by in range(1, members):
            copies.start(
                z_slots[by - 1], gathered.at[first, xpos, ypos],
                gathered.at[first + members - by, xpos, ypos], along_z(by, members),
            )
        ring_slots = [[(copies.slot(), copies.slot()) for _ in range(1, SIDE)] for _ in groups]
        next_slots = [
            [[(copies.slot(), copies.slot()) for _ in range(1, SIDE)] for _ in range(1, SIDE)] for _ in groups
        ]

        def to_rings(g):
            where = pl.ds(*groups[g])
            block = gathered.at[where, xpos, ypos]
            for by in range(1, SIDE):
                copies.start(ring_slots[g][by - 1][0], block, block, along_x(by))
                copies.start(ring_slots[g][by - 1][1], block, block, along_y(by))

        def onward(g):
            where = pl.ds(*groups[g])
            for by in range(1, SIDE):
                x_from, y_from = lax.rem(xpos + SIDE - by, SIDE), lax.rem(ypos + SIDE - by, SIDE)
                copies.arrived(ring_slots[g][by - 1][0], gathered.at[where, x_from, ypos], along_x(by))
                block = gathered.at[where, x_from, ypos, 0:HALF]
                for on in range(1, SIDE):
                    copies.start(next_slots[g][by - 1][on - 1][0], block, block, along_y(on))
                copies.arrived(ring_slots[g][by - 1][1], gathered.at[where, xpos, y_from], along_y(by))
                block = gathered.at[where, xpos, y_from, HALF:ROWS]
                for on in range(1, SIDE):
                    copies.start(next_slots[g][by - 1][on - 1][1], block, block, along_x(on))

        def all_in(g):
            where = pl.ds(*groups[g])
            for by in range(1, SIDE):
                for on in range(1, SIDE):
                    x_from, y_from = lax.rem(xpos + SIDE - by, SIDE), lax.rem(ypos + SIDE - on, SIDE)
                    copies.arrived(
                        next_slots[g][by - 1][on - 1][0], gathered.at[where, x_from, y_from, 0:HALF], along_y(on)
                    )
                    x_from, y_from = lax.rem(xpos + SIDE - on, SIDE), lax.rem(ypos + SIDE - by, SIDE)
                    copies.arrived(
                        next_slots[g][by - 1][on - 1][1], gathered.at[where, x_from, y_from, HALF:ROWS], along_x(on)
                    )

        def multiply(d):
            vectors = gathered[first + d].reshape(BLOCK, COLS)
            both = jnp.concatenate(split(vectors), 1)
            blk = first + lax.rem(member + d, members)
            return jnp.dot(rows_cat[blk], both, preferred_element_type=F32)

        to_rings(0)
        early()
        if members > 1:
            for by in range(1, members):
                copies.arrived(
                    z_slots[by - 1], gathered.at[first + members - by, xpos, ypos], along_z(by, members)
                )
            to_rings(1)
        for g in range(len(groups)):
            onward(g)
        late()
        all_in(0)
        total = multiply(0)
        if members > 1:
            all_in(1)
            for d in range(1, members):
                total = total + multiply(d)
        total = total[:, :COLS] + total[:, COLS:]
        total = total[: 2 * ROWS] + total[2 * ROWS :]
        cross[k, 0] = total[ROWS:]
        slot = copies.slot()
        copies.start(slot, cross.at[k, 0], cross.at[k, 1], sibling)
        copies.arrived(slot, cross.at[k, 1], sibling)
        return total[:ROWS] + cross[k, 1]

    def spread_product(k, shard):
        first, members = FIRST[k], COUNT[k]
        member = lax.rem(cube, members)
        mine[k, 0] = shard
        slot = copies.slot()
        copies.start(slot, mine.at[k, 0], mine.at[k, 1], sibling)
        copies.arrived(slot, mine.at[k, 1], sibling)
        high, low = split(mine[k].reshape(2 * ROWS, COLS))
        vectors = jnp.concatenate([high, low], 1)
        vectors = jnp.concatenate([vectors, vectors], 0)
        groups = ([(first + 1, members - 1)] if members > 1 else []) + [(first, 1)]
        first_slots = [[(copies.slot(), copies.slot()) for _ in range(1, SIDE)] for _ in groups]
        second_slots = [[(copies.slot(), copies.slot()) for _ in range(1, SIDE)] for _ in groups]
        z_slots = [copies.slot() for _ in range(1, members)]

        for g, (begin, size) in enumerate(groups):
            for d in range(begin - first, begin - first + size):
                blk = first + lax.rem(member + d, members)
                product = jnp.dot(cols_cat[blk], vectors, preferred_element_type=F32)
                product = product[:, :COLS] + product[:, COLS:]
                partial[first + d] = product.reshape(SIDE, SIDE, ROWS, COLS)
            where = pl.ds(begin, size)
            for by in range(1, SIDE):
                copies.start(
                    first_slots[g][by - 1][0], partial.at[where, :, lax.rem(ypos + by, SIDE), 0:HALF],
                    recv_first.at[0, by - 1, where], along_y(by),
                )
                copies.start(
                    first_slots[g][by - 1][1], partial.at[where, lax.rem(xpos + by, SIDE), :, HALF:ROWS],
                    recv_first.at[1, by - 1, where], along_x(by),
                )

        for g, (begin, size) in enumerate(groups):
            where = pl.ds(begin, size)
            for by in range(1, SIDE):
                copies.arrived(first_slots[g][by - 1][0], recv_first.at[0, by - 1, where], along_y(by))
                copies.arrived(first_slots[g][by - 1][1], recv_first.at[1, by - 1, where], along_x(by))
            for b in range(begin, begin + size):
                upper = partial[b, :, ypos, 0:HALF]
                lower = partial[b, xpos, :, HALF:ROWS]
                for by in range(SIDE - 1):
                    upper = upper + recv_first[0, by, b]
                    lower = lower + recv_first[1, by, b]
                reduced[0, b] = upper
                reduced[1, b] = lower
            for by in range(1, SIDE):
                copies.start(
                    second_slots[g][by - 1][0], reduced.at[0, where, lax.rem(xpos + by, SIDE)],
                    recv_second.at[by - 1, where, 0:HALF], along_x(by),
                )
                copies.start(
                    second_slots[g][by - 1][1], reduced.at[1, where, lax.rem(ypos + by, SIDE)],
                    recv_second.at[by - 1, where, HALF:ROWS], along_y(by),
                )

        for g, (begin, size) in enumerate(groups):
            where = pl.ds(begin, size)
            for by in range(1, SIDE):
                copies.arrived(second_slots[g][by - 1][0], recv_second.at[by - 1, where, 0:HALF], along_x(by))
                copies.arrived(second_slots[g][by - 1][1], recv_second.at[by - 1, where, HALF:ROWS], along_y(by))
            for b in range(begin, begin + size):
                total = jnp.concatenate([reduced[0, b, xpos], reduced[1, b, ypos]], 0)
                for by in range(SIDE - 1):
                    total = total + recv_second[by, b]
                if b == first:
                    own = total
                else:
                    by = b - first
                    recv_cube[0, b] = total
                    copies.start(z_slots[by - 1], recv_cube.at[0, b], recv_cube.at[1, b], along_z(by, members))
        for by in range(1, members):
            copies.arrived(z_slots[by - 1], recv_cube.at[1, first + by], along_z(by, members))
            own = own + recv_cube[1, first + by]
        return own

    def nothing():
        pass

    def all_of(*steps):
        def run():
            for step, *which in steps:
                step(*which)

        return run

    solved_leaf = gather_product(
        0, sides[0, 0],
        all_of((halve, 0, None), (halve, 1, pmid), (halve, 2, None)),
        all_of((halve, 3, ptop), (halve, 4, None), (fill_rows, 0)),
    )
    update_mid = gather_product(1, solved_leaf, all_of((fill_rows, 1)), all_of((fill_rows, 2)))
    solved_mid = gather_product(2, sides[1, 0] - update_mid, nothing, all_of((fill_rows, 3), (fill_cols, 0)))
    update_top = gather_product(3, solved_mid, nothing, all_of((fill_rows, 4), (fill_cols, 1), (fill_cols, 2)))
    solved_top = gather_product(4, sides[2, 0] - update_top, nothing, all_of((fill_cols, 4), (fill_cols, 3)))
    back_top = spread_product(4, solved_top)
    out[2, 0] = back_top
    carry_mid = spread_product(3, back_top)
    back_mid = spread_product(2, solved_mid - carry_mid)
    out[1, 0] = back_mid
    carry_leaf = spread_product(1, back_mid)
    back_leaf = spread_product(0, solved_leaf - carry_leaf)
    out[0, 0] = back_leaf
    copies.finish()


def local(right_sides, inverse_leaf, inverse_mid, inverse_top, coupling_mid, coupling_top, pattern_mid, pattern_top):
    n_copies = 420
    vmem = pl.BlockSpec(memory_space=pltpu.VMEM)
    smem = pl.BlockSpec(memory_space=pltpu.SMEM)
    hbm = pl.BlockSpec(memory_space=pl.ANY)
    return pl.pallas_call(
        kernel,
        out_shape=jax.ShapeDtypeStruct(right_sides.shape, F32),
        in_specs=[vmem, hbm, hbm, hbm, hbm, hbm, smem, smem],
        out_specs=vmem,
        scratch_shapes=[
            *[pltpu.VMEM((ROWS, 2 * BLOCK * count), F32) for count in COUNT],
            pltpu.VMEM((2, BLOCKS, ROWS, BLOCK), F32),
            pltpu.VMEM((BLOCKS, ROWS, BLOCK), F32),
            pltpu.VMEM((BLOCKS, 4 * ROWS, BLOCK), BF16),
            pltpu.VMEM((BLOCKS, BLOCK, 4 * ROWS), BF16),
            pltpu.VMEM((BLOCKS, SIDE, SIDE, ROWS, COLS), F32),
            pltpu.VMEM((BLOCKS, SIDE, SIDE, ROWS, COLS), F32),
            pltpu.VMEM((2, SIDE - 1, BLOCKS, SIDE, HALF, COLS), F32),
            pltpu.VMEM((SIDE - 1, BLOCKS, ROWS, COLS), F32),
            pltpu.VMEM((2, BLOCKS, SIDE, HALF, COLS), F32),
            pltpu.VMEM((2, BLOCKS, ROWS, COLS), F32),
            pltpu.VMEM((5, 2, ROWS, COLS), F32),
            pltpu.VMEM((5, 2, ROWS, COLS), F32),
            pltpu.SemaphoreType.DMA((5,)),
            pltpu.SemaphoreType.DMA((n_copies,)),
            pltpu.SemaphoreType.DMA((n_copies,)),
        ],
        compiler_params=pltpu.CompilerParams(
            collective_id=0, has_side_effects=True, vmem_limit_bytes=62 * 2**20
        ),
        name="solve",
    )(right_sides, inverse_leaf, inverse_mid, inverse_top, coupling_mid, coupling_top, pattern_mid, pattern_top)


def solution(mesh):
    split_rows = P("cube", "front", None)
    levels = P(None, "cube", "front", None)
    return jax.shard_map(
        local, mesh=mesh, in_specs=(levels,) + (split_rows,) * 7, out_specs=levels, check_vma=False,
    )
```

time: 986 us -> 179 us (0.18)
  waiting for transfers between devices: 831 us -> 0 us
  Pallas kernels: 0 us -> 178 us
  matrix products: 53.5 us -> 0 us
  starting transfers between devices: 51.8 us -> 0 us
  local copies, waits for them, and re-layouts: 21.7 us -> 1.54 us
  between operations: 14.2 us -> 0.01 us
    reduce_scatter x9 -> x0, waiting for transfers between devices: 572 us -> none  [the longest x5 444 us: spread_back(): lax.psum_scatter(jnp.einsum('rms,rn->smn', shaped, local_rows, precision=...]
    all_gather x5 -> x0, waiting for transfers between devices: 255 us -> none  [gathered_product(): lax.all_gather(stacked, 'front', axis=1, tiled=True)]
    pallas_call x0 -> x1, Pallas kernels: none -> 178 us  [local(): pl.pallas_call(kernel, out_shape=jax.ShapeDtypeStruct(right_sides.shape,...]
    dot_general x10 -> x0, matrix products: 53.5 us -> none  [the longest x5 32.6 us: spread_back(): jnp.einsum('rms,rn->smn', shaped, local_rows, precision=lax.Precision.HIG...]
    ppermute x16 -> x0, starting transfers between devices: 50.1 us -> none  [from_behind(): return lax.ppermute(array, axis, pairs)]
  transfers between devices with their start and end apart: 30 -> 0, of which waited for: 18 -> 0; matrix products, arithmetic and copies ran while one was open for 1% -> 0% of each run, Pallas kernels for 0% -> 0%
where the time goes in v1:
time: 179 us
  Pallas kernels  178 us (99%)
    pallas_call x1, Pallas kernels, local(): pl.pallas_call(kernel, out_shape=jax.ShapeDtypeStruct(right_sides.shape,...  178 us

profile of v1, /device:TPU:1, one launch (start us, length us, event | category | flops | bytes accessed | tf_op | source)
XLA Modules:
  0.0 179.1 jit_solution(3602807492029357806)
XLA Ops:
  0.0 177.5 %solve.1 = f32[3,1,64,128]{3,2,1,0:T(8,128)} custom-call(f32[3,1,64,128]{3,2,1,0:T(8,128)} %sides.1, f32[1,64,2048]{2,1,0:T(8,128)} %leaf.1, f32[1,64,4096]{2,1,0:T(8,128)} %mid.1, f32[1,64,8192]{2,1,0:T(8,128)} %top.1, f32[1,64,4096]{2,1,0:T(8,128)} %cmid.1, f32[1,64,8192]{2,1,0:T(8,128)} %ctop.1, s32[1,1,64]{2,1,0:T(1,128)} %pmid.1, s32[1,1,128]{2,1,0:T(1,128)} %ptop.1), custom_call_target="tpu_custom_call" | custom-call | tf_op jit(solution)/shard_map/solve/pallas_call | solution.py:343
  177.5 1.5 copy.10

commit v2 on v1

v2 whole, which is shorter than its diff:
```python
import functools

import jax
import jax.numpy as jnp
from jax import lax
from jax.experimental import pallas as pl
from jax.experimental.pallas import tpu as pltpu
from jax.sharding import PartitionSpec as P

MESH = pl.DeviceIdType.MESH
SIDE = 4
ROWS = 64
COLS = 128
CHAINS = 2
PACK = ROWS // CHAINS
HALF = PACK // 2
BLOCK = SIDE * SIDE * ROWS
FIRST = (0, 1, 3, 5, 9)
COUNT = (1, 2, 2, 4, 4)
BLOCKS = 13
LAG = 1
F32, BF16 = jnp.float32, jnp.bfloat16


def split(values):
    high = values.astype(BF16)
    low = (values - high.astype(F32)).astype(BF16)
    return high, low


def left_lanes(values):
    return lax.broadcasted_iota(jnp.int32, values.shape, values.ndim - 1) < COLS // 2


def side_by_side(packed):
    flat = packed.reshape(-1, COLS)
    turned = pltpu.roll(flat, COLS // 2, 1)
    left = left_lanes(flat)
    high, low = flat.astype(BF16).astype(F32), turned - turned.astype(BF16).astype(F32)
    upper = jnp.where(left, high, low).astype(BF16)
    high, low = turned.astype(BF16).astype(F32), flat - flat.astype(BF16).astype(F32)
    lower = jnp.where(left, high, low).astype(BF16)
    both = jnp.concatenate([upper.reshape(packed.shape), lower.reshape(packed.shape)], 1)
    return both.reshape(-1, COLS)


def packed_sum(product):
    total = (product + pltpu.roll(product, COLS // 2, 1)).reshape(-1, ROWS, COLS)
    upper, lower = total[:, :PACK], total[:, PACK:]
    return jnp.where(left_lanes(upper), upper, lower)


def packed(values, chain):
    upper, lower = values[:PACK], values[PACK:]
    if chain == 0:
        return jnp.where(left_lanes(upper), upper, pltpu.roll(lower, COLS // 2, 1))
    return jnp.where(left_lanes(upper), pltpu.roll(upper, COLS // 2, 1), lower)


def unpacked(first, second):
    left = left_lanes(first)
    upper = jnp.where(left, first, pltpu.roll(second, COLS // 2, 1))
    lower = jnp.where(left, pltpu.roll(first, COLS // 2, 1), second)
    return jnp.concatenate([upper, lower], 0)


class Copies:
    def __init__(self, send, recv):
        self.send, self.recv, self.used = send, recv, 0

    def slot(self):
        self.used += 1
        assert self.used <= RECEIVE
        return self.used - 1

    def start(self, group, slot, src, dst, device):
        pltpu.make_async_remote_copy(
            src_ref=src, dst_ref=dst, send_sem=self.send.at[group], recv_sem=self.recv.at[slot],
            device_id=device, device_id_type=MESH,
        ).start()

    def arrived(self, slot, dst, device):
        pltpu.make_async_remote_copy(
            src_ref=dst, dst_ref=dst, send_sem=self.send.at[0], recv_sem=self.recv.at[slot],
            device_id=device, device_id_type=MESH,
        ).wait_recv()

    def all_sent(self, group, as_many, device):
        pltpu.make_async_remote_copy(
            src_ref=as_many, dst_ref=as_many, send_sem=self.send.at[group], recv_sem=self.recv.at[0],
            device_id=device, device_id_type=MESH,
        ).wait_send()


SENDS = CHAINS * 10 + 1
RECEIVE = 203


def kernel(
    sides, leaf, mid, top, cmid, ctop, pmid, ptop, out,
    raw_leaf, raw_cmid, raw_mid, raw_ctop, raw_top, halves, sibling_half, rows_cat, cols_cat,
    gathered, partial, recv_first, recv_second, reduced, recv_cube, mine, cross, result, local_sem, send, recv,
):
    cube = lax.axis_index("cube")
    front = lax.axis_index("front")
    core = lax.rem(front, 2)
    ypos = lax.rem(front // 2, SIDE)
    xpos = front // (2 * SIDE)

    def at(x, y, z, c):
        return (z, (x * SIDE + y) * 2 + c)

    def along_x(by):
        return at(lax.rem(xpos + by, SIDE), ypos, cube, core)

    def along_y(by):
        return at(xpos, lax.rem(ypos + by, SIDE), cube, core)

    def along_z(by, members):
        member = lax.rem(cube, members)
        return at(xpos, ypos, cube - member + lax.rem(member + by, members), core)

    sibling = at(xpos, ypos, cube, 1 - core)
    copies = Copies(send, recv)

    raws = (raw_leaf, raw_cmid, raw_mid, raw_ctop, raw_top)
    loads = []
    for k, (src, dst) in enumerate(zip((leaf, cmid, mid, ctop, top), raws)):
        load = pltpu.make_async_copy(src.at[0], dst, local_sem.at[k])
        load.start()
        loads.append(load)

    barrier = pltpu.get_barrier_semaphore()
    peers = [sibling]
    for by in range(1, SIDE):
        peers += [along_x(by), along_y(by), along_z(by, 4)]
    for peer in peers:
        pl.semaphore_signal(barrier, inc=1, device_id=peer, device_id_type=MESH)
    pl.semaphore_wait(barrier, len(peers))

    lane = lax.broadcasted_iota(jnp.int32, (ROWS, 128), 1)
    first_half = lane < ROWS

    half_slots = {}

    def halve(k, pattern):
        loads[k].wait()

        def one(m, carry):
            for i in range(BLOCK // 128):
                at_column = pl.multiple_of(m * (2 * BLOCK) + i * 256, 256)
                left = raws[k][:, pl.ds(at_column, 128)]
                right = raws[k][:, pl.ds(at_column + 128, 128)]
                low = jnp.where(first_half, left, pltpu.roll(right, ROWS, 1))
                high = jnp.where(first_half, pltpu.roll(left, ROWS, 1), right)
                if pattern is not None:
                    tile = m * (2 * BLOCK // ROWS) + 4 * i
                    keep = [pattern[0, 0, tile + j].astype(F32) for j in range(4)]
                    low = low * jnp.where(first_half, keep[0], keep[2])
                    high = high * jnp.where(first_half, keep[1], keep[3])
                halves[0, FIRST[k] + m, :, i * 128 : (i + 1) * 128] = low
                halves[1, FIRST[k] + m, :, i * 128 : (i + 1) * 128] = high
            return carry

        lax.fori_loop(0, COUNT[k], one, 0)
        where = pl.ds(FIRST[k], COUNT[k])
        half_slots[k] = copies.slot()
        copies.start(SENDS - 1, half_slots[k], halves.at[1 - core, where], sibling_half.at[where], sibling)

    def fill_rows(k):
        copies.arrived(half_slots[k], sibling_half.at[pl.ds(FIRST[k], COUNT[k])], sibling)

        def one(m, carry):
            blk = FIRST[k] + m
            for first, source in ((0, halves[core, blk]), (ROWS, sibling_half[blk])):
                high, low = split(source)
                rows_cat[blk, first : first + ROWS] = high
                rows_cat[blk, 2 * ROWS + first : 3 * ROWS + first] = low
            return carry

        lax.fori_loop(0, COUNT[k], one, 0)

    def fill_cols(k):
        def one(m, carry):
            blk = FIRST[k] + m
            for i in range(BLOCK // 128):
                part = slice(i * 128, (i + 1) * 128)
                both = jnp.concatenate([halves[core, blk, :, part], sibling_half[blk, :, part]], 0)
                high, low = split(both.T)
                cols_cat[blk, part, :128] = high
                cols_cat[blk, part, 128:] = low
            return carry

        lax.fori_loop(0, COUNT[k], one, 0)

    def gather_product(c, k, shard, early=None, late=None):
        first, members = FIRST[k], COUNT[k]
        member = lax.rem(cube, members)
        group = c * 10 + k
        gathered[c, first, xpos, ypos] = shard
        groups = [(first, 1)] + ([(first + 1, members - 1)] if members > 1 else [])
        z_slot = copies.slot() if members > 1 else None
        for by in range(1, members):
            copies.start(
                group, z_slot, gathered.at[c, first, xpos, ypos],
                gathered.at[c, first + members - by, xpos, ypos], along_z(by, members),
            )
        ring_slots = [[(copies.slot(), copies.slot()) for _ in range(1, SIDE)] for _ in groups]
        next_slots = [copies.slot() for _ in groups]

        def to_rings(g):
            where = pl.ds(*groups[g])
            block = gathered.at[c, where, xpos, ypos]
            for by in range(1, SIDE):
                copies.start(group, ring_slots[g][by - 1][0], block, block, along_x(by))
                copies.start(group, ring_slots[g][by - 1][1], block, block, along_y(by))

        def onward(g):
            where = pl.ds(*groups[g])
            for by in (1, 3, 2):
                x_from, y_from = lax.rem(xpos + SIDE - by, SIDE), lax.rem(ypos + SIDE - by, SIDE)
                copies.arrived(ring_slots[g][by - 1][0], gathered.at[c, where, x_from, ypos], along_x(by))
                block = gathered.at[c, where, x_from, ypos, 0:HALF]
                for on in range(1, SIDE):
                    copies.start(group, next_slots[g], block, block, along_y(on))
                copies.arrived(ring_slots[g][by - 1][1], gathered.at[c, where, xpos, y_from], along_y(by))
                block = gathered.at[c, where, xpos, y_from, HALF:PACK]
                for on in range(1, SIDE):
                    copies.start(group, next_slots[g], block, block, along_x(on))

        def multiply(d):
            vectors = side_by_side(gathered[c, first + d].reshape(SIDE * SIDE, PACK, COLS))
            blk = first + lax.rem(member + d, members)
            return jnp.dot(rows_cat[blk], vectors, preferred_element_type=F32)

        to_rings(0)
        if early:
            early()
        yield
        if members > 1:
            copies.arrived(z_slot, gathered.at[c, pl.ds(first + 1, members - 1), xpos, ypos], sibling)
            to_rings(1)
            yield
        for g in range(len(groups)):
            onward(g)
        if late:
            late()
        yield
        total = None
        for g, (begin, size) in enumerate(groups):
            copies.arrived(next_slots[g], gathered.at[c, pl.ds(begin, size), 0 : SIDE - 1, 0 : SIDE - 1], sibling)
            for d in range(begin - first, begin - first + size):
                term = multiply(d)
                total = term if total is None else total + term
        total = packed_sum(total[: 2 * ROWS] + total[2 * ROWS :])
        cross[c, k, 0] = total[1]
        slot = copies.slot()
        copies.start(group, slot, cross.at[c, k, 0], cross.at[c, k, 1], sibling)
        copies.arrived(slot, cross.at[c, k, 1], sibling)
        return total[0] + cross[c, k, 1]

    def spread_product(c, k, shard):
        first, members = FIRST[k], COUNT[k]
        member = lax.rem(cube, members)
        group = c * 10 + 5 + k
        mine[c, k, 0] = shard
        slot = copies.slot()
        copies.start(group, slot, mine.at[c, k, 0], mine.at[c, k, 1], sibling)
        groups = ([(first + 1, members - 1)] if members > 1 else []) + [(first, 1)]
        first_slots = [copies.slot() for _ in groups]
        second_slots = [copies.slot() for _ in groups]
        z_slot = copies.slot() if members > 1 else None
        copies.arrived(slot, mine.at[c, k, 1], sibling)
        vectors = side_by_side(mine[c, k])
        vectors = jnp.concatenate([vectors, vectors], 0)
        for g, (begin, size) in enumerate(groups):
            for d in range(begin - first, begin - first + size):
                blk = first + lax.rem(member + d, members)
                product = packed_sum(jnp.dot(cols_cat[blk], vectors, preferred_element_type=F32))
                partial[c, first + d] = product.reshape(SIDE, SIDE, PACK, COLS)
            where = pl.ds(begin, size)
            for by in range(1, SIDE):
                copies.start(
                    group, first_slots[g], partial.at[c, where, :, lax.rem(ypos + by, SIDE), 0:HALF],
                    recv_first.at[c, 0, by - 1, where], along_y(by),
                )
                copies.start(
                    group, first_slots[g], partial.at[c, where, lax.rem(xpos + by, SIDE), :, HALF:PACK],
                    recv_first.at[c, 1, by - 1, where], along_x(by),
                )
        yield
        for g, (begin, size) in enumerate(groups):
            where = pl.ds(begin, size)
            copies.arrived(first_slots[g], recv_first.at[c, :, :, where], sibling)
            for b in range(begin, begin + size):
                upper = partial[c, b, :, ypos, 0:HALF]
                lower = partial[c, b, xpos, :, HALF:PACK]
                for by in range(SIDE - 1):
                    upper = upper + recv_first[c, 0, by, b]
                    lower = lower + recv_first[c, 1, by, b]
                reduced[c, 0, b] = upper
                reduced[c, 1, b] = lower
            for by in range(1, SIDE):
                copies.start(
                    group, second_slots[g], reduced.at[c, 0, where, lax.rem(xpos + by, SIDE)],
                    recv_second.at[c, by - 1, where, 0:HALF], along_x(by),
                )
                copies.start(
                    group, second_slots[g], reduced.at[c, 1, where, lax.rem(ypos + by, SIDE)],
                    recv_second.at[c, by - 1, where, HALF:PACK], along_y(by),
                )
        yield
        for g, (begin, size) in enumerate(groups):
            where = pl.ds(begin, size)
            copies.arrived(second_slots[g], recv_second.at[c, :, where], sibling)
            for b in range(begin, begin + size):
                total = jnp.concatenate([reduced[c, 0, b, xpos], reduced[c, 1, b, ypos]], 0)
                for by in range(SIDE - 1):
                    total = total + recv_second[c, by, b]
                if b == first:
                    own = total
                else:
                    recv_cube[c, 0, b] = total
                    copies.start(group, z_slot, recv_cube.at[c, 0, b], recv_cube.at[c, 1, b], along_z(b - first, members))
        if members > 1:
            yield
            copies.arrived(z_slot, recv_cube.at[c, 1, pl.ds(first + 1, members - 1)], sibling)
            for by in range(1, members):
                own = own + recv_cube[c, 1, first + by]
        return own

    def all_of(*steps):
        def run():
            for step, *which in steps:
                step(*which)

        return run

    def chain(c):
        def when_first(*steps):
            return all_of(*steps) if c == 0 else None

        solved_leaf = yield from gather_product(
            c, 0, packed(sides[0, 0], c), when_first((halve, 0, None), (halve, 1, pmid)),
            when_first((halve, 2, None), (fill_rows, 0)),
        )
        update_mid = yield from gather_product(
            c, 1, solved_leaf, when_first((fill_rows, 1),), when_first((halve, 3, ptop), (fill_rows, 2))
        )
        solved_mid = yield from gather_product(
            c, 2, packed(sides[1, 0], c) - update_mid, None, when_first((halve, 4, None), (fill_rows, 3))
        )
        update_top = yield from gather_product(
            c, 3, solved_mid, None, when_first((fill_rows, 4), (fill_cols, 0), (fill_cols, 1), (fill_cols, 2))
        )
        solved_top = yield from gather_product(
            c, 4, packed(sides[2, 0], c) - update_top, None, when_first((fill_cols, 4), (fill_cols, 3))
        )
        result[c, 2] = yield from spread_product(c, 4, solved_top)
        carry_mid = yield from spread_product(c, 3, result[c, 2])
        result[c, 1] = yield from spread_product(c, 2, solved_mid - carry_mid)
        carry_leaf = yield from spread_product(c, 1, result[c, 1])
        result[c, 0] = yield from spread_product(c, 0, solved_leaf - carry_leaf)

    chains = [chain(c) for c in range(CHAINS)]
    for _ in range(LAG):
        next(chains[0])
    done = object()
    while chains:
        chains = [one for one in reversed(chains) if next(one, done) is not done][::-1]
    for level in range(3):
        out[level, 0] = unpacked(result[0, level], result[1, level])
    copies.all_sent(SENDS - 1, sibling_half, sibling)
    for c in range(CHAINS):
        for k in range(5):
            where = pl.ds(FIRST[k], COUNT[k])
            copies.all_sent(c * 10 + k, gathered.at[c, where], sibling)
            copies.all_sent(c * 10 + 5 + k, partial.at[c, where], sibling)


def local(right_sides, inverse_leaf, inverse_mid, inverse_top, coupling_mid, coupling_top, pattern_mid, pattern_top):
    vmem = pl.BlockSpec(memory_space=pltpu.VMEM)
    smem = pl.BlockSpec(memory_space=pltpu.SMEM)
    hbm = pl.BlockSpec(memory_space=pl.ANY)
    return pl.pallas_call(
        kernel,
        out_shape=jax.ShapeDtypeStruct(right_sides.shape, F32),
        in_specs=[vmem, hbm, hbm, hbm, hbm, hbm, smem, smem],
        out_specs=vmem,
        scratch_shapes=[
            *[pltpu.VMEM((ROWS, 2 * BLOCK * count), F32) for count in COUNT],
            pltpu.VMEM((2, BLOCKS, ROWS, BLOCK), F32),
            pltpu.VMEM((BLOCKS, ROWS, BLOCK), F32),
            pltpu.VMEM((BLOCKS, 4 * ROWS, BLOCK), BF16),
            pltpu.VMEM((BLOCKS, BLOCK, 4 * ROWS), BF16),
            pltpu.VMEM((CHAINS, BLOCKS, SIDE, SIDE, PACK, COLS), F32),
            pltpu.VMEM((CHAINS, BLOCKS, SIDE, SIDE, PACK, COLS), F32),
            pltpu.VMEM((CHAINS, 2, SIDE - 1, BLOCKS, SIDE, HALF, COLS), F32),
            pltpu.VMEM((CHAINS, SIDE - 1, BLOCKS, PACK, COLS), F32),
            pltpu.VMEM((CHAINS, 2, BLOCKS, SIDE, HALF, COLS), F32),
            pltpu.VMEM((CHAINS, 2, BLOCKS, PACK, COLS), F32),
            pltpu.VMEM((CHAINS, 5, 2, PACK, COLS), F32),
            pltpu.VMEM((CHAINS, 5, 2, PACK, COLS), F32),
            pltpu.VMEM((CHAINS, 3, PACK, COLS), F32),
            pltpu.SemaphoreType.DMA((5,)),
            pltpu.SemaphoreType.DMA((SENDS,)),
            pltpu.SemaphoreType.DMA((RECEIVE,)),
        ],
        compiler_params=pltpu.CompilerParams(
            collective_id=0, has_side_effects=True, vmem_limit_bytes=62 * 2**20
        ),
        name="solve",
    )(right_sides, inverse_leaf, inverse_mid, inverse_top, coupling_mid, coupling_top, pattern_mid, pattern_top)


def solution(mesh):
    split_rows = P("cube", "front", None)
    levels = P(None, "cube", "front", None)
    return jax.shard_map(
        local, mesh=mesh, in_specs=(levels,) + (split_rows,) * 7, out_specs=levels, check_vma=False,
    )
```

time: 179 us -> 159 us (0.89)
  Pallas kernels: 178 us -> 157 us
    pallas_call x1, Pallas kernels: 178 us -> 157 us  [local(): pl.pallas_call(kernel, out_shape=jax.ShapeDtypeStruct(right_sides.shape,...]
where the time goes in v2:
time: 159 us; the launch traced here: 158 us
  Pallas kernels  157 us (99%)
    pallas_call x1, Pallas kernels, local(): pl.pallas_call(kernel, out_shape=jax.ShapeDtypeStruct(right_sides.shape,...  157 us

profile of v2, /device:TPU:1, one launch (start us, length us, event | category | flops | bytes accessed | tf_op | source)
XLA Modules:
  0.0 158.4 jit_solution(11600710110725740719)
XLA Ops:
  0.0 156.9 %solve.1 = f32[3,1,64,128]{3,2,1,0:T(8,128)} custom-call(f32[3,1,64,128]{3,2,1,0:T(8,128)} %sides.1, f32[1,64,2048]{2,1,0:T(8,128)} %leaf.1, f32[1,64,4096]{2,1,0:T(8,128)} %mid.1, f32[1,64,8192]{2,1,0:T(8,128)} %top.1, f32[1,64,4096]{2,1,0:T(8,128)} %cmid.1, f32[1,64,8192]{2,1,0:T(8,128)} %ctop.1, s32[1,1,64]{2,1,0:T(1,128)} %pmid.1, s32[1,1,128]{2,1,0:T(1,128)} %ptop.1), custom_call_target="tpu_custom_call" | custom-call | tf_op jit(solution)/shard_map/solve/pallas_call | solution.py:385
  156.9 1.5 copy.10

commit v3 on v2

--- a/solution.py
+++ b/solution.py
@@ -18,6 +18,7 @@
 FIRST = (0, 1, 3, 5, 9)
 COUNT = (1, 2, 2, 4, 4)
 BLOCKS = 13
+TURNS = ((1, 3), (2,))
 LAG = 1
 F32, BF16 = jnp.float32, jnp.bfloat16
 
@@ -93,7 +94,7 @@
 
 
 SENDS = CHAINS * 10 + 1
-RECEIVE = 203
+RECEIVE = 131
 
 
 def kernel(
@@ -205,28 +206,28 @@
                 group, z_slot, gathered.at[c, first, xpos, ypos],
                 gathered.at[c, first + members - by, xpos, ypos], along_z(by, members),
             )
-        ring_slots = [[(copies.slot(), copies.slot()) for _ in range(1, SIDE)] for _ in groups]
+        ring_slots = [[copies.slot() for _ in TURNS] for _ in groups]
         next_slots = [copies.slot() for _ in groups]
 
         def to_rings(g):
             where = pl.ds(*groups[g])
             block = gathered.at[c, where, xpos, ypos]
-            for by in range(1, SIDE):
-                copies.start(group, ring_slots[g][by - 1][0], block, block, along_x(by))
-                copies.start(group, ring_slots[g][by - 1][1], block, block, along_y(by))
+            for slot, turn in zip(ring_slots[g], TURNS):
+                for by in turn:
+                    copies.start(group, slot, block, block, along_x(by))
+                    copies.start(group, slot, block, block, along_y(by))
 
         def onward(g):
             where = pl.ds(*groups[g])
-            for by in (1, 3, 2):
-                x_from, y_from = lax.rem(xpos + SIDE - by, SIDE), lax.rem(ypos + SIDE - by, SIDE)
-                copies.arrived(ring_slots[g][by - 1][0], gathered.at[c, where, x_from, ypos], along_x(by))
-                block = gathered.at[c, where, x_from, ypos, 0:HALF]
-                for on in range(1, SIDE):
-                    copies.start(group, next_slots[g], block, block, along_y(on))
-                copies.arrived(ring_slots[g][by - 1][1], gathered.at[c, where, xpos, y_from], along_y(by))
-                block = gathered.at[c, where, xpos, y_from, HALF:PACK]
-                for on in range(1, SIDE):
-                    copies.start(group, next_slots[g], block, block, along_x(on))
+            for slot, turn in zip(ring_slots[g], TURNS):
+                copies.arrived(slot, gathered.at[c, where, 0 : 2 * len(turn), ypos], sibling)
+                for by in turn:
+                    x_from, y_from = lax.rem(xpos + SIDE - by, SIDE), lax.rem(ypos + SIDE - by, SIDE)
+                    block_x = gathered.at[c, where, x_from, ypos, 0:HALF]
+                    block_y = gathered.at[c, where, xpos, y_from, HALF:PACK]
+                    for on in (1, 3, 2):
+                        copies.start(group, next_slots[g], block_x, block_x, along_y(on))
+                        copies.start(group, next_slots[g], block_y, block_y, along_x(on))
 
         def multiply(d):
             vectors = side_by_side(gathered[c, first + d].reshape(SIDE * SIDE, PACK, COLS))
@@ -240,9 +241,9 @@
         if members > 1:
             copies.arrived(z_slot, gathered.at[c, pl.ds(first + 1, members - 1), xpos, ypos], sibling)
             to_rings(1)
+            onward(0)
             yield
-        for g in range(len(groups)):
-            onward(g)
+        onward(len(groups) - 1)
         if late:
             late()
         yield
@@ -311,6 +312,8 @@
                 )
         yield
         for g, (begin, size) in enumerate(groups):
+            if g:
+                yield
             where = pl.ds(begin, size)
             copies.arrived(second_slots[g], recv_second.at[c, :, where], sibling)
             for b in range(begin, begin + size):
@@ -323,7 +326,6 @@
                     recv_cube[c, 0, b] = total
                     copies.start(group, z_slot, recv_cube.at[c, 0, b], recv_cube.at[c, 1, b], along_z(b - first, members))
         if members > 1:
-            yield
             copies.arrived(z_slot, recv_cube.at[c, 1, pl.ds(first + 1, members - 1)], sibling)
             for by in range(1, members):
                 own = own + recv_cube[c, 1, first + by]
@@ -341,8 +343,8 @@
             return all_of(*steps) if c == 0 else None
 
         solved_leaf = yield from gather_product(
-            c, 0, packed(sides[0, 0], c), when_first((halve, 0, None), (halve, 1, pmid)),
-            when_first((halve, 2, None), (fill_rows, 0)),
+            c, 0, packed(sides[0, 0], c), when_first((halve, 0, None),),
+            when_first((halve, 1, pmid), (fill_rows, 0), (halve, 2, None)),
         )
         update_mid = yield from gather_product(
             c, 1, solved_leaf, when_first((fill_rows, 1),), when_first((halve, 3, ptop), (fill_rows, 2))

time: 159 us -> 158 us (level)
  no operation moved by 1% of the time
where the time goes in v3:
time: 158 us; the launch traced here: 157 us
  Pallas kernels  156 us (99%)
    pallas_call x1, Pallas kernels, local(): pl.pallas_call(kernel, out_shape=jax.ShapeDtypeStruct(right_sides.shape,...  156 us

profile of v3, /device:TPU:1, one launch (start us, length us, event | category | flops | bytes accessed | tf_op | source)
XLA Modules:
  0.0 157.5 jit_solution(14390583315084523434)
XLA Ops:
  0.0 155.9 %solve.1 = f32[3,1,64,128]{3,2,1,0:T(8,128)} custom-call(f32[3,1,64,128]{3,2,1,0:T(8,128)} %sides.1, f32[1,64,2048]{2,1,0:T(8,128)} %leaf.1, f32[1,64,4096]{2,1,0:T(8,128)} %mid.1, f32[1,64,8192]{2,1,0:T(8,128)} %top.1, f32[1,64,4096]{2,1,0:T(8,128)} %cmid.1, f32[1,64,8192]{2,1,0:T(8,128)} %ctop.1, s32[1,1,64]{2,1,0:T(1,128)} %pmid.1, s32[1,1,128]{2,1,0:T(1,128)} %ptop.1), custom_call_target="tpu_custom_call" | custom-call | tf_op jit(solution)/shard_map/solve/pallas_call | solution.py:387
  155.9 1.5 copy.10

commit v4 on v3

--- a/solution.py
+++ b/solution.py
@@ -173,10 +173,10 @@
 
         def one(m, carry):
             blk = FIRST[k] + m
-            for first, source in ((0, halves[core, blk]), (ROWS, sibling_half[blk])):
+            for first, source in ((0, halves[core, blk]), (2 * ROWS, sibling_half[blk])):
                 high, low = split(source)
                 rows_cat[blk, first : first + ROWS] = high
-                rows_cat[blk, 2 * ROWS + first : 3 * ROWS + first] = low
+                rows_cat[blk, first + ROWS : first + 2 * ROWS] = low
             return carry
 
         lax.fori_loop(0, COUNT[k], one, 0)
@@ -229,10 +229,10 @@
                         copies.start(group, next_slots[g], block_x, block_x, along_y(on))
                         copies.start(group, next_slots[g], block_y, block_y, along_x(on))
 
-        def multiply(d):
+        def multiply(d, rows):
             vectors = side_by_side(gathered[c, first + d].reshape(SIDE * SIDE, PACK, COLS))
             blk = first + lax.rem(member + d, members)
-            return jnp.dot(rows_cat[blk], vectors, preferred_element_type=F32)
+            return jnp.dot(rows_cat[blk, rows], vectors, preferred_element_type=F32)
 
         to_rings(0)
         if early:
@@ -247,18 +247,24 @@
         if late:
             late()
         yield
-        total = None
+        own, other = slice(0, 2 * ROWS), slice(2 * ROWS, 4 * ROWS)
+        total = jnp.zeros((4 * ROWS, COLS), F32)
         for g, (begin, size) in enumerate(groups):
             copies.arrived(next_slots[g], gathered.at[c, pl.ds(begin, size), 0 : SIDE - 1, 0 : SIDE - 1], sibling)
             for d in range(begin - first, begin - first + size):
-                term = multiply(d)
-                total = term if total is None else total + term
-        total = packed_sum(total[: 2 * ROWS] + total[2 * ROWS :])
-        cross[c, k, 0] = total[1]
+                if d < members - 1:
+                    total = total + multiply(d, slice(0, 4 * ROWS))
+
+        def last(rows):
+            part = total[rows] + multiply(members - 1, rows)
+            return packed_sum(part[:ROWS] + part[ROWS:])[0]
+
+        cross[c, k, 0] = last(other)
         slot = copies.slot()
         copies.start(group, slot, cross.at[c, k, 0], cross.at[c, k, 1], sibling)
+        mine_now = last(own)
         copies.arrived(slot, cross.at[c, k, 1], sibling)
-        return total[0] + cross[c, k, 1]
+        return mine_now + cross[c, k, 1]
 
     def spread_product(c, k, shard):
         first, members = FIRST[k], COUNT[k]

time: 158 us -> 158 us (level)
  no operation moved by 1% of the time
where the time goes in v4:
time: 158 us
  Pallas kernels  157 us (99%)
    pallas_call x1, Pallas kernels, local(): pl.pallas_call(kernel, out_shape=jax.ShapeDtypeStruct(right_sides.shape,...  157 us

profile of v4, /device:TPU:1, one launch (start us, length us, event | category | flops | bytes accessed | tf_op | source)
XLA Modules:
  0.0 158.1 jit_solution(638909166478264198)
XLA Ops:
  0.0 156.6 %solve.1 = f32[3,1,64,128]{3,2,1,0:T(8,128)} custom-call(f32[3,1,64,128]{3,2,1,0:T(8,128)} %sides.1, f32[1,64,2048]{2,1,0:T(8,128)} %leaf.1, f32[1,64,4096]{2,1,0:T(8,128)} %mid.1, f32[1,64,8192]{2,1,0:T(8,128)} %top.1, f32[1,64,4096]{2,1,0:T(8,128)} %cmid.1, f32[1,64,8192]{2,1,0:T(8,128)} %ctop.1, s32[1,1,64]{2,1,0:T(1,128)} %pmid.1, s32[1,1,128]{2,1,0:T(1,128)} %ptop.1), custom_call_target="tpu_custom_call" | custom-call | tf_op jit(solution)/shard_map/solve/pallas_call | solution.py:393
  156.6 1.5 copy.10

commit v5 on v3

--- a/solution.py
+++ b/solution.py
@@ -194,7 +194,7 @@
 
         lax.fori_loop(0, COUNT[k], one, 0)
 
-    def gather_product(c, k, shard, early=None, late=None):
+    def gather_product(c, k, shard, early=None, late=None, beside=None):
         first, members = FIRST[k], COUNT[k]
         member = lax.rem(cube, members)
         group = c * 10 + k
@@ -257,6 +257,8 @@
         cross[c, k, 0] = total[1]
         slot = copies.slot()
         copies.start(group, slot, cross.at[c, k, 0], cross.at[c, k, 1], sibling)
+        if beside:
+            beside()
         copies.arrived(slot, cross.at[c, k, 1], sibling)
         return total[0] + cross[c, k, 1]
 
@@ -342,21 +344,24 @@
         def when_first(*steps):
             return all_of(*steps) if c == 0 else None
 
+        def beside(first_steps, second_steps):
+            return all_of(*(second_steps if c else first_steps))
+
         solved_leaf = yield from gather_product(
-            c, 0, packed(sides[0, 0], c), when_first((halve, 0, None),),
-            when_first((halve, 1, pmid), (fill_rows, 0), (halve, 2, None)),
+            c, 0, packed(sides[0, 0], c), when_first((halve, 0, None)), when_first((halve, 1, pmid), (fill_rows, 0)),
+            beside([(halve, 2, None)], [(halve, 3, ptop)]),
         )
         update_mid = yield from gather_product(
-            c, 1, solved_leaf, when_first((fill_rows, 1),), when_first((halve, 3, ptop), (fill_rows, 2))
+            c, 1, solved_leaf, None, when_first((fill_rows, 1)), beside([(halve, 4, None)], [(fill_rows, 2)])
         )
         solved_mid = yield from gather_product(
-            c, 2, packed(sides[1, 0], c) - update_mid, None, when_first((halve, 4, None), (fill_rows, 3))
+            c, 2, packed(sides[1, 0], c) - update_mid, None, None, beside([(fill_rows, 3)], [(fill_rows, 4)])
         )
         update_top = yield from gather_product(
-            c, 3, solved_mid, None, when_first((fill_rows, 4), (fill_cols, 0), (fill_cols, 1), (fill_cols, 2))
+            c, 3, solved_mid, None, None, beside([(fill_cols, 4)], [(fill_cols, 2), (fill_cols, 1)])
         )
         solved_top = yield from gather_product(
-            c, 4, packed(sides[2, 0], c) - update_top, None, when_first((fill_cols, 4), (fill_cols, 3))
+            c, 4, packed(sides[2, 0], c) - update_top, None, None, beside([(fill_cols, 3)], [(fill_cols, 0)])
         )
         result[c, 2] = yield from spread_product(c, 4, solved_top)
         carry_mid = yield from spread_product(c, 3, result[c, 2])

time: 158 us -> 161 us (1.019)
  Pallas kernels: 156 us -> 159 us
    pallas_call x1, Pallas kernels: 156 us -> 159 us  [local(): pl.pallas_call(kernel, out_shape=jax.ShapeDtypeStruct(right_sides.shape,...]
where the time goes in v5:
time: 161 us
  Pallas kernels  159 us (99%)
    pallas_call x1, Pallas kernels, local(): pl.pallas_call(kernel, out_shape=jax.ShapeDtypeStruct(right_sides.shape,...  159 us

profile of v5, /device:TPU:1, one launch (start us, length us, event | category | flops | bytes accessed | tf_op | source)
XLA Modules:
  0.0 160.7 jit_solution(1581608270444184746)
XLA Ops:
  0.0 159.1 %solve.1 = f32[3,1,64,128]{3,2,1,0:T(8,128)} custom-call(f32[3,1,64,128]{3,2,1,0:T(8,128)} %sides.1, f32[1,64,2048]{2,1,0:T(8,128)} %leaf.1, f32[1,64,4096]{2,1,0:T(8,128)} %mid.1, f32[1,64,8192]{2,1,0:T(8,128)} %top.1, f32[1,64,4096]{2,1,0:T(8,128)} %cmid.1, f32[1,64,8192]{2,1,0:T(8,128)} %ctop.1, s32[1,1,64]{2,1,0:T(1,128)} %pmid.1, s32[1,1,128]{2,1,0:T(1,128)} %ptop.1), custom_call_target="tpu_custom_call" | custom-call | tf_op jit(solution)/shard_map/solve/pallas_call | solution.py:392
  159.1 1.5 copy.10
